TPU v7x, 32 devices: a whole 2x2x4 slice. The times are simulated.
32 devices in a mesh: row: 8 (over z, y), col: 4 (over x, core).
Axes of the slice: x: 2, y: 2, z: 4, core: 2. Of those that a mesh axis runs over, the one named last changes fastest.
Arguments:
- features: bfloat16 [4, 4096, 128], P('col', 'row'), may hold values from -6 to 6
- weight1: bfloat16 [128, 128], replicated, may hold values from -0.5 to 0.5
- weight2: bfloat16 [128, 128], replicated, may hold values from -0.5 to 0.5
- tile_values: bfloat16 [8, 4, 96, 128, 128], P('row', 'col'), may hold values from -0.375 to 0.375
- tile_coords: int32 [8, 4, 2, 96], P('row', 'col'), may hold values from 0 to 31, as said below
- tile_count: int32 [8, 4], P('row', 'col'), may hold values from 1 to 96, as said below
- out_grad: bfloat16 [4, 4096, 128], P('col', 'row'), may hold values from -6 to 6
Outputs:
- output: bfloat16 [4, 4096, 128], P('col', 'row')
- grad_features: bfloat16 [4, 4096, 128], P('col', 'row')
- grad_weight1: float32 [128, 128], replicated
- grad_weight2: float32 [128, 128], replicated
Inputs may be any that keep to these rules, and one draw needn't show every extreme that they name: On each device tile_coords[r, c, 0, t] is below 16 and tile_coords[r, c, 1, t] below 32; no block position appears twice among a device's 96 slots. `tile_count`: some device has all 96 slots live.
All inputs are finite; a program needn't handle non-finite values.
Results may differ from a plain program's by a relative error of at most 0.034.
Values may be sent and summed in bfloat16 or wider, within the bound.
A program may use at most 64 MiB of HBM per device.

v0:
```python
import math

import jax
import jax.numpy as jnp
from jax import lax
from jax.sharding import PartitionSpec as P


def forward_part(local_tiles, row_ids, col_ids, live_slots, panel_rows, row_blocks):
    block_side = local_tiles.shape[1]
    feat_width = panel_rows.shape[-1]
    blocks = panel_rows.reshape(-1, block_side, feat_width)[col_ids]
    products = jnp.einsum("tij,tjf->tif", local_tiles, blocks, preferred_element_type=jnp.float32)
    onehot = jnp.where(
        (row_ids[None, :] == jnp.arange(row_blocks, dtype=jnp.int32)[:, None])
        & live_slots[None, :],
        1.0,
        0.0,
    ).astype(jnp.float32)
    return jnp.einsum("rt,tif->rif", onehot, products).reshape(row_blocks * block_side, feat_width)


def transposed_part(local_tiles, row_ids, col_ids, live_slots, panel_rows, col_blocks):
    block_side = local_tiles.shape[1]
    feat_width = panel_rows.shape[-1]
    blocks = panel_rows.reshape(-1, block_side, feat_width)[row_ids]
    products = jnp.einsum("tji,tjf->tif", local_tiles, blocks, preferred_element_type=jnp.float32)
    onehot = jnp.where(
        (col_ids[None, :] == jnp.arange(col_blocks, dtype=jnp.int32)[:, None])
        & live_slots[None, :],
        1.0,
        0.0,
    ).astype(jnp.float32)
    return jnp.einsum("ct,tif->cif", onehot, products).reshape(col_blocks * block_side, feat_width)


def silu_slope(value):
    sigmoid = jax.nn.sigmoid(value)
    return sigmoid * (1.0 + value * (1.0 - sigmoid))


def on_device(features, weight1, weight2, tile_values, tile_coords, tile_count, out_grad):
    local_tiles = tile_values[0, 0]
    row_ids = tile_coords[0, 0, 0]
    col_ids = tile_coords[0, 0, 1]
    slot_total = local_tiles.shape[0]
    live_slots = jnp.arange(slot_total, dtype=jnp.int32) < tile_count[0, 0]
    block_side = local_tiles.shape[1]
    shard_rows = features.shape[1]
    row_blocks = shard_rows * lax.axis_size("col") // block_side
    col_blocks = shard_rows * lax.axis_size("row") // block_side
    node_total = shard_rows * lax.axis_size("row") * lax.axis_size("col")
    grad_local = out_grad[0]
    grad_two = jnp.dot(grad_local, weight2.T, preferred_element_type=jnp.float32).astype(
        jnp.bfloat16
    )
    gathered = lax.all_gather(features, "row", axis=1, tiled=True)[0]
    grad_rows = lax.all_gather(grad_two, "row", axis=0, tiled=True)
    part_one = forward_part(local_tiles, row_ids, col_ids, live_slots, gathered, row_blocks)
    part_three = forward_part(local_tiles, row_ids, col_ids, live_slots, grad_rows, row_blocks)
    agg_sum, grad_hidden = (
        lax.psum_scatter(
            part_one.astype(jnp.bfloat16), "col", scatter_dimension=0, tiled=True
        ).astype(jnp.float32),
        lax.psum_scatter(
            part_three.astype(jnp.bfloat16), "col", scatter_dimension=0, tiled=True
        ).astype(jnp.float32),
    )
    agg_one = agg_sum.astype(jnp.bfloat16)
    pre_one = jnp.dot(agg_one, weight1, preferred_element_type=jnp.float32)
    hidden = jax.nn.silu(pre_one).astype(jnp.bfloat16)
    hidden_rows = lax.all_gather(hidden, "col", axis=0, tiled=True)
    part_two = transposed_part(local_tiles, row_ids, col_ids, live_slots, hidden_rows, col_blocks)
    agg_two = lax.psum_scatter(
        part_two.astype(jnp.bfloat16), "row", scatter_dimension=0, tiled=True
    )
    output = jnp.dot(agg_two, weight2, preferred_element_type=jnp.float32).astype(jnp.bfloat16)
    grad_pre = (grad_hidden * silu_slope(pre_one)).astype(jnp.bfloat16)
    grad_one = jnp.dot(grad_pre, weight1.T, preferred_element_type=jnp.float32).astype(jnp.bfloat16)
    grad_hidden_rows = lax.all_gather(grad_one, "col", axis=0, tiled=True)
    part_four = transposed_part(
        local_tiles, row_ids, col_ids, live_slots, grad_hidden_rows, col_blocks
    )
    grad_features = lax.psum_scatter(
        part_four.astype(jnp.bfloat16), "row", scatter_dimension=0, tiled=True
    )
    contract = (((0,), (0,)), ((), ()))
    weight_one = lax.dot_general(agg_one, grad_pre, contract, preferred_element_type=jnp.float32)
    weight_two = lax.dot_general(agg_two, grad_local, contract, preferred_element_type=jnp.float32)
    sum_one, sum_two = lax.psum((weight_one, weight_two), ("row", "col"))
    factor = 1.0 / math.sqrt(node_total)
    return (output[None], grad_features[None], sum_one * factor, sum_two * factor)


def solution(mesh):
    placed = (
        P("col", "row", None),
        P(),
        P(),
        P("row", "col", None, None, None),
        P("row", "col", None, None),
        P("row", "col"),
        P("col", "row", None),
    )
    return jax.shard_map(
        on_device,
        mesh=mesh,
        in_specs=placed,
        out_specs=(P("col", "row", None), P("col", "row", None), P(), P()),
        check_vma=False,
    )
```

profile of v0, /device:TPU:0, one launch (start us, length us, event | category | flops | bytes accessed | tf_op | source)
XLA Modules:
  0.0 434.1 jit_solution(17749796915655797008)
XLA Ops:
  7.2 0.0 all-gather.3.cloned.1.call-start
  7.2 0.7 all-gather.3.cloned.1.call-update
  7.9 0.0 all-gather.5.cloned.1.call-start
  8.0 1.9 convolution_convert_fusion.1
  9.9 0.0 all-gather.5.cloned.1.call-update
  9.9 0.0 reduce-scatter.5.cloned.1.call-start
  10.6 0.8 fusion.63
  11.4 0.8 slice_bitcast_fusion.1
  12.1 40.9 %all-gather.3.cloned.1.call-done = bf16[1,4096,128]{2,1,0:T(8,128)(2,1)} async-done(((bf16[1,512,128]{2,1,0:T(8,128)(2,1)}), bf16[1,4096,128]{2,1,0:T(8,128)(2,1)}) %all-gather.3.cloned.1.call-update) | async-done | bytes 1048592 | tf_op jit(solution)/shard_map/all_gather | solution.py:57
  53.0 3.9 gather_fusion
  56.9 5.9 %fusion.14 = bf16[96,128,128]{2,1,0:T(8,128)(2,1)} fusion(bf16[96,128,128]{2,1,0:T(8,128)(2,1)} %gather_fusion, bf16[1,1,96,128,128]{4,3,2,1,0:T(8,128)(2,1)S(1)} %copy-done), kind=kOutput, calls=%fused_computation.18 | convolution fusion | flops 402653184 | bytes 9437184 | tf_op jit(solution)/shard_map/tij,tjf->tif/dot_general | solution.py:13
  62.9 5.0 %copy.16 = bf16[96,128,128]{1,0,2:T(8,128)(2,1)} copy(bf16[96,128,128]{2,1,0:T(8,128)(2,1)} %fusion.14) | data formatting | bytes 6291456 | tf_op jit(solution)/shard_map/tij,tjf->tif/dot_general | solution.py:13
  67.8 2.4 fusion.22
  70.2 1.0 copy.12
  71.2 0.0 reduce-scatter.5.cloned.1.call-update
  71.2 0.0 reduce-scatter.9.cloned.1.call-start
  71.3 23.5 %all-gather.5.cloned.1.call-done = bf16[4096,128]{1,0:T(8,128)(2,1)} async-done(((bf16[512,128]{1,0:T(8,128)(2,1)}), bf16[4096,128]{1,0:T(8,128)(2,1)}) %all-gather.5.cloned.1.call-update) | async-done | bytes 1048592 | tf_op jit(solution)/shard_map/all_gather | solution.py:58
  94.7 3.9 gather_fusion.2
  98.6 5.9 %fusion.10 = bf16[96,128,128]{2,1,0:T(8,128)(2,1)} fusion(bf16[96,128,128]{2,1,0:T(8,128)(2,1)} %gather_fusion.2, bf16[1,1,96,128,128]{4,3,2,1,0:T(8,128)(2,1)S(1)} %copy-done), kind=kOutput, calls=%fused_computation.14 | convolution fusion | flops 402653184 | bytes 9437184 | tf_op jit(solution)/shard_map/tij,tjf->tif/dot_general | solution.py:13
  104.6 5.0 %copy.18 = bf16[96,128,128]{1,0,2:T(8,128)(2,1)} copy(bf16[96,128,128]{2,1,0:T(8,128)(2,1)} %fusion.10) | data formatting | bytes 6291456 | tf_op jit(solution)/shard_map/tij,tjf->tif/dot_general | solution.py:13
  109.5 2.4 fusion.25
  111.9 1.0 copy.14
  112.9 0.0 reduce-scatter.7.cloned.1.call-start
  113.0 4.7 %reduce-scatter.5.cloned.1.call-done = bf16[512,128]{1,0:T(8,128)(2,1)} async-done(((bf16[2048,128]{1,0:T(8,128)(2,1)}), bf16[512,128]{1,0:T(8,128)(2,1)}) %reduce-scatter.5.cloned.1.call-update) | async-done | bytes 131088 | tf_op jit(solution)/shard_map/reduce_scatter | solution.py:62
  117.6 24.2 %reduce-scatter.9.cloned.1.call-done = bf16[512,128]{1,0:T(8,128)(2,1)} async-done(((bf16[2048,128]{1,0:T(8,128)(2,1)}), bf16[512,128]{1,0:T(8,128)(2,1)}) %reduce-scatter.9.cloned.1.call-update) | async-done | bytes 131088 | tf_op jit(solution)/shard_map/reduce_scatter | solution.py:65
  141.8 1.2 multiply_convert_fusion
  143.1 7.2 %all_gather.13 = bf16[2048,128]{1,0:T(8,128)(2,1)} all-gather(bf16[512,128]{1,0:T(8,128)(2,1)S(1)} %get-tuple-element.7), channel_id=1, replica_groups=mesh['row'=8,'col'=4] {'col'}, dimensions={0}, use_global_device_ids=true | all-gather | bytes 655360 | tf_op jit(solution)/shard_map/all_gather | solution.py:72
  150.3 3.7 gather_fusion.1
  154.0 4.8 %fusion.12 = bf16[96,128,128]{2,1,0:T(8,128)(2,1)} fusion(bf16[96,128,128]{2,1,0:T(8,128)(2,1)} %gather_fusion.1, bf16[1,1,96,128,128]{4,3,2,1,0:T(8,128)(2,1)S(1)} %copy-done), kind=kOutput, calls=%fused_computation.16 | convolution fusion | flops 402653184 | bytes 9437184 | tf_op jit(solution)/shard_map/tji,tjf->tif/dot_general | solution.py:27
  158.8 5.0 %copy.17 = bf16[96,128,128]{1,0,2:T(8,128)(2,1)} copy(bf16[96,128,128]{2,1,0:T(8,128)(2,1)} %fusion.12) | data formatting | bytes 6291456 | tf_op jit(solution)/shard_map/tji,tjf->tif/dot_general | solution.py:27
  163.8 2.4 fusion.16
  166.2 1.4 copy.13
  167.6 0.0 all-reduce.3.cloned.1.call-start
  167.7 0.2 convolution_convert_fusion
  167.9 7.9 %all_gather.15 = bf16[2048,128]{1,0:T(8,128)(2,1)} all-gather(bf16[512,128]{1,0:T(8,128)(2,1)S(1)} %convolution_convert_fusion), channel_id=1, replica_groups=mesh['row'=8,'col'=4] {'col'}, dimensions={0}, use_global_device_ids=true | all-gather | bytes 655360 | tf_op jit(solution)/shard_map/all_gather | solution.py:80
  175.8 3.7 gather_fusion.3
  179.5 4.8 %fusion.8 = bf16[96,128,128]{2,1,0:T(8,128)(2,1)} fusion(bf16[96,128,128]{2,1,0:T(8,128)(2,1)} %gather_fusion.3, bf16[1,1,96,128,128]{4,3,2,1,0:T(8,128)(2,1)S(1)} %copy-done), kind=kOutput, calls=%fused_computation.12 | convolution fusion | flops 402653184 | bytes 9437184 | tf_op jit(solution)/shard_map/tji,tjf->tif/dot_general | solution.py:27
  184.3 5.0 %copy.19 = bf16[96,128,128]{1,0,2:T(8,128)(2,1)} copy(bf16[96,128,128]{2,1,0:T(8,128)(2,1)} %fusion.8) | data formatting | bytes 6291456 | tf_op jit(solution)/shard_map/tji,tjf->tif/dot_general | solution.py:27
  189.4 0.9 fusion.72
  190.2 41.3 %reduce-scatter.7.cloned.1.call-done = bf16[512,128]{1,0:T(8,128)(2,1)} async-done(((bf16[4096,128]{1,0:T(8,128)(2,1)}), bf16[512,128]{1,0:T(8,128)(2,1)}) %reduce-scatter.7.cloned.1.call-update) | async-done | bytes 131088 | tf_op jit(solution)/shard_map/reduce_scatter | solution.py:74
  231.5 1.8 fusion.29
  233.3 0.0 reduce-scatter.11.cloned.1.call-start
  233.3 2.4 fusion.19
  235.8 1.4 copy.15
  237.2 0.8 fusion.28
  238.0 122.4 %all-reduce.3.cloned.1.call-done = (f32[128,128]{1,0:T(8,128)}, f32[128,128]{1,0:T(8,128)}) async-done(((f32[128,128]{1,0:T(8,128)}, f32[128,128]{1,0:T(8,128)}), (f32[128,128]{1,0:T(8,128)}, f32[128,128]{1,0:T(8,128)})) %all-reduce.3.cloned.1.call-update) | async-done | bytes 131088 | tf_op jit(solution)/shard_map/psum | solution.py:90
  360.4 1.5 broadcast_multiply_fusion
  362.0 65.3 %reduce-scatter.11.cloned.1.call-done = bf16[512,128]{1,0:T(8,128)(2,1)} async-done(((bf16[4096,128]{1,0:T(8,128)(2,1)}), bf16[512,128]{1,0:T(8,128)(2,1)}) %reduce-scatter.11.cloned.1.call-update) | async-done | bytes 131088 | tf_op jit(solution)/shard_map/reduce_scatter | solution.py:84
  (19 shorter events, 0.1 us)
Async XLA Ops:
  7.2 49.8 %copy-start = (bf16[1,1,96,128,128]{4,3,2,1,0:T(8,128)(2,1)S(1)}, bf16[1,1,96,128,128]{4,3,2,1,0:T(8,128)(2,1)}, u32[]{:S(2)}) copy-start(bf16[1,1,96,128,128]{4,3,2,1,0:T(8,128)(2,1)} %param.10) | copy-start | bytes 9437188
  7.2 45.8 %all-gather.3.cloned.1.call-start = ((), (), s32[]{:S(2)}) async-start(), calls=%async_computation.4 | async-start | bytes 1179648 | tf_op jit(solution)/shard_map/all_gather | solution.py:57
  7.9 86.8 %all-gather.5.cloned.1.call-start = ((), (), s32[]{:S(2)}) async-start(), calls=%async_computation.7 | async-start | bytes 1179648 | tf_op jit(solution)/shard_map/all_gather | solution.py:58
  9.9 107.7 %reduce-scatter.5.cloned.1.call-start = ((), (), s32[]{:S(2)}) async-start(), calls=%async_computation.5 | async-start | bytes 655360 | tf_op jit(solution)/shard_map/reduce_scatter | solution.py:62
  71.2 70.6 %reduce-scatter.9.cloned.1.call-start = ((), (), s32[]{:S(2)}) async-start(), calls=%async_computation.8 | async-start | bytes 655360 | tf_op jit(solution)/shard_map/reduce_scatter | solution.py:65
  109.5 32.3 %copy-start.5 = (bf16[128,128]{1,0:T(8,128)(2,1)S(1)}, bf16[128,128]{1,0:T(8,128)(2,1)}, u32[]{:S(2)}) copy-start(bf16[128,128]{1,0:T(8,128)(2,1)} %param.8) | copy-start | bytes 98308
  112.9 118.5 %reduce-scatter.7.cloned.1.call-start = ((), (), s32[]{:S(2)}) async-start(), calls=%async_computation.6 | async-start | bytes 1179648 | tf_op jit(solution)/shard_map/reduce_scatter | solution.py:74
  167.6 192.8 %all-reduce.3.cloned.1.call-start = ((), (), s32[]{:S(2)}) async-start(), calls=%async_computation.10 | async-start | bytes 262144 | tf_op jit(solution)/shard_map/psum | solution.py:90
  184.3 5.0 %copy-start.4 = (bf16[512,128]{1,0:T(8,128)(2,1)S(1)}, bf16[512,128]{1,0:T(8,128)(2,1)}, u32[]{:S(2)}) copy-start(bf16[512,128]{1,0:T(8,128)(2,1)} %reduce-scatter.5.cloned.1.call-done) | copy-start | bytes 393220
  184.3 47.1 %copy-start.1 = (bf16[1,512,128]{2,1,0:T(8,128)(2,1)S(1)}, bf16[1,512,128]{2,1,0:T(8,128)(2,1)}, u32[]{:S(2)}) copy-start(bf16[1,512,128]{2,1,0:T(8,128)(2,1)} %param.13) | copy-start | bytes 393220
  233.3 3.9 copy-start.2
  233.3 3.9 copy-start.3
  233.3 194.0 %reduce-scatter.11.cloned.1.call-start = ((), (), s32[]{:S(2)}) async-start(), calls=%async_computation.9 | async-start | bytes 1179648 | tf_op jit(solution)/shard_map/reduce_scatter | solution.py:84
Sparse Core Ops, SparseCore 0:
  10.1 42.8 all-gather.2
  55.7 38.9 all-gather.4
  97.2 20.3 reduce-scatter.4
  120.1 21.6 reduce-scatter.8
  167.8 63.6 reduce-scatter.6
  238.6 121.8 all-reduce.2
  364.8 62.4 reduce-scatter.10
where the time goes:
time: 435 us; the launch traced here: 434 us
  waiting for transfers between devices  323 us (74%)
  local copies, waits for them, and re-layouts  40.7 us (9%)
  matrix products  37.9 us (9%)
  blocking collectives  15.1 us (3%)
  between operations  14.9 us (3%)
    psum x1, waiting for transfers between devices, on_device(): sum_one, sum_two = lax.psum((weight_one, weight_two), ('row', 'col'))  122 us
    reduce_scatter x1, waiting for transfers between devices, on_device(): lax.psum_scatter(part_four.astype(jnp.bfloat16), 'row', scatter_dimension...  65.3 us
    reduce_scatter x1, waiting for transfers between devices, on_device(): lax.psum_scatter(part_two.astype(jnp.bfloat16), 'row', scatter_dimension=...  41.3 us
    all_gather x1, waiting for transfers between devices, on_device(): gathered = lax.all_gather(features, 'row', axis=1, tiled=True)[0]  40.9 us
    reduce_scatter x1, waiting for transfers between devices, on_device(): lax.psum_scatter(part_three.astype(jnp.bfloat16), 'col', scatter_dimensio...  24.2 us
    all_gather x1, waiting for transfers between devices, on_device(): grad_rows = lax.all_gather(grad_two, 'row', axis=0, tiled=True)  23.5 us
    dot_general x2, matrix products, forward_part(): jnp.einsum('tij,tjf->tif', local_tiles, blocks, preferred_element_type=jn...  11.8 us
    dot_general x2, local copies, waits for them, and re-layouts, transposed_part(): jnp.einsum('tji,tjf->tif', local_tiles, blocks, preferred_element_type=jn...  9.98 us
  transfers between devices with their start and end apart: 7, of which 7 were waited for; matrix products, arithmetic and copies ran while one was open for 14% of the time, Pallas kernels for 0%

commit v1 on v0

v1 whole, which is shorter than its diff:
```python
import functools
import math

import jax
import jax.numpy as jnp
from jax import lax
from jax.experimental import pallas as pl
from jax.experimental.pallas import tpu as pltpu
from jax.sharding import PartitionSpec as P

MESH = pl.DeviceIdType.MESH
BF16 = jnp.bfloat16
F32 = jnp.float32


def dot(a, b, dims=((1,), (0,))):
    return lax.dot_general(a, b, (dims, ((), ())), preferred_element_type=F32)


def kernel(
    nr, nc, factor,
    slot_ref, feat_ref, grad_ref, w1_ref, w2_ref, tiles_hbm,
    out_ref, gf_ref, gw1_ref, gw2_ref,
    tiles, dense, xs, part, psend, precv, pre, hid, agg, zt,
    ybuf, yrecv, zbuf, zrecv, gsend, grecv, gsum, gfin,
    tile_sem, xss, xrs, pss, prs, tss, trs, yss, yrs, zss, zrs,
    g1s, g1r, g2s, g2r, g3s, g3r,
):
    shard, width = feat_ref.shape
    blk = tiles.shape[1]
    panel = dense.shape[1]
    n_tiles = tiles.shape[0] - 1
    zn = nr // 2
    r, c = lax.axis_index("row"), lax.axis_index("col")
    z, y = r // 2, r % 2
    mate = z * 2 + (1 - y)
    piece = 2 * width // nc

    tile_copy = pltpu.make_async_copy(tiles_hbm, tiles.at[pl.ds(0, n_tiles)], tile_sem)
    tile_copy.start()
    xs[0, r] = feat_ref[...]
    xs[1, r] = grad_ref[...]

    barrier = pltpu.get_barrier_semaphore()

    def greet(axis, n, me):
        def body(k, _):
            pl.semaphore_signal(barrier, inc=1, device_id={axis: (me + k) % n}, device_id_type=MESH)
            return 0
        lax.fori_loop(1, n, body, 0)
    greet("row", nr, r)
    greet("col", nc, c)
    pl.semaphore_wait(barrier, nr - 1 + nc - 1)

    def remote(src, dst, ss, rs, axis, target):
        return pltpu.make_async_remote_copy(
            src_ref=src, dst_ref=dst, send_sem=ss, recv_sem=rs,
            device_id={axis: target}, device_id_type=MESH)

    def x_copy(h, idx, way):
        target = (r + 2, r - 2, mate)[way]
        return remote(xs.at[h, idx], xs.at[h, idx], xss.at[h, idx, way], xrs.at[h, idx], "row", target)

    def x_forward(h, idx, sign, act):
        @pl.when(sign > 0)
        def _():
            @pl.when(z < zn - 1)
            def _():
                act(x_copy(h, idx, 0))

        @pl.when(sign < 0)
        def _():
            @pl.when(z > 0)
            def _():
                act(x_copy(h, idx, 1))

    def start(copy):
        copy.start()

    def wait_send(copy):
        copy.wait_send()

    def x_own(h, act):
        act(x_copy(h, r, 2))

        @pl.when(z < zn - 1)
        def _():
            act(x_copy(h, r, 0))

        @pl.when(z > 0)
        def _():
            act(x_copy(h, r, 1))

    rows_step = 512

    def accumulate(h, idx, first=False):
        def body(m, _):
            rows = pl.ds(pl.multiple_of(m * rows_step, rows_step), rows_step)
            add = dot(dense[idx, rows, :], xs[h, idx])
            part[h, rows, :] = add if first else part[h, rows, :] + add
            return 0
        lax.fori_loop(0, panel // rows_step, body, 0)

    def x_pass(h, s):
        def body(q, _):
            sign = 1 - 2 * q
            zz = z - sign * s

            @pl.when((zz >= 0) & (zz < zn))
            def _():
                idx = zz * 2 + y
                x_copy(h, idx, 2).wait_recv()
                x_forward(h, idx, sign, start)
                x_copy(h, idx, 2).start()
            return 0
        lax.fori_loop(0, 2, body, 0)

    def x_use(h, s):
        def body(q, _):
            late = q // 2
            sign = 2 * (q % 2) - 1
            zz = z + sign * (s - late)
            yy = y + late * (1 - 2 * y)

            @pl.when((zz >= 0) & (zz < zn) & ((q < 3) | (s > 1)))
            def _():
                idx = zz * 2 + yy

                @pl.when(late == 1)
                def _():
                    x_copy(h, idx, 2).wait_recv()
                accumulate(h, idx)
            return 0
        lax.fori_loop(0, 4, body, 0)

    def x_steps(h, lo, hi):
        def body(s, _):
            x_pass(h, s)
            x_use(h, s)
            return 0
        lax.fori_loop(lo, hi, body, 0)

    def x_drain(h):
        x_own(h, wait_send)

        def body(k, _):
            q, s = k % 2, k // 2 + 1
            sign = 1 - 2 * q
            zz = z - sign * s

            @pl.when((zz >= 0) & (zz < zn))
            def _():
                idx = zz * 2 + y
                x_forward(h, idx, sign, wait_send)
                x_copy(h, idx, 2).wait_send()
            return 0
        lax.fori_loop(0, 2 * (zn - 1), body, 0)

    def peers(n, me, act):
        def body(k, _):
            act((me + k) % n)
            return 0
        lax.fori_loop(1, n, body, 0)

    def p_copy(h, peer, src):
        return remote(psend.at[h, peer], precv.at[h, src], pss.at[h, peer], prs.at[h, src], "col", peer)

    def own_rows():
        return pl.ds(pl.multiple_of(c * shard, shard), shard)

    def p_send(h):
        def act(peer):
            rows = pl.ds(pl.multiple_of(peer * shard, shard), shard)
            psend[h, peer] = part[h, rows, :].astype(BF16)
            p_copy(h, peer, c).start()
        peers(nc, c, act)

    def p_sum(h):
        agg[h] = part[h, own_rows(), :].astype(BF16).astype(F32)

        def act(peer):
            p_copy(h, peer, peer).wait_recv()
            agg[h] = agg[h] + precv[h, peer].astype(F32)
        peers(nc, c, act)
        return agg[h]

    def t_copy(h, peer, src):
        return remote(zt.at[h, src], zt.at[h, src], tss.at[h, peer], trs.at[h, src], "col", peer)

    def z_send(h, value):
        zt[h, c] = value.T.astype(BF16)
        peers(nc, c, lambda peer: t_copy(h, peer, c).start())

    def z_wait(h):
        peers(nc, c, lambda peer: t_copy(h, peer, peer).wait_recv())

    def product(h, idx):
        total = dot(zt[h, 0], dense[idx, 0:shard, :])
        for k in range(1, nc):
            total = total + dot(zt[h, k], dense[idx, k * shard:(k + 1) * shard, :])
        return total

    def y_copy(h, zd):
        return remote(ybuf.at[h, zd], yrecv.at[h, zd], yss.at[h, zd], yrs.at[h, zd], "row", mate)

    def z_copy(h, zd, side):
        target = (r + 2, r - 2)[side]
        return remote(zbuf.at[h, zd], zrecv.at[h, side, zd], zss.at[h, zd], zrs.at[h, side, zd], "row", target)

    def both(d, act):
        def body(q, _):
            zd = z + (2 * q - 1) * d

            @pl.when((zd >= 0) & (zd < zn) & ((q == 0) | (d > 0)))
            def _():
                act(zd)
            return 0
        lax.fori_loop(0, 2, body, 0)

    def y_part(h, d):
        def act(zd):
            ybuf[h, zd] = product(h, zd * 2 + (1 - y)).astype(BF16)
            y_copy(h, zd).start()
        both(d, act)

    def z_part(h, d, total):
        def act(zd):
            total[...] = product(h, zd * 2 + y)
            y_copy(h, zd).wait_recv()
            total[...] = total[...] + yrecv[h, zd].astype(F32)

            @pl.when((z > 0) & (zd >= z))
            def _():
                z_copy(h, zd, 0).wait_recv()
                total[...] = total[...] + zrecv[h, 0, zd].astype(F32)

            @pl.when((z < zn - 1) & (zd <= z))
            def _():
                z_copy(h, zd, 1).wait_recv()
                total[...] = total[...] + zrecv[h, 1, zd].astype(F32)

            @pl.when(zd != z)
            def _():
                zbuf[h, zd] = total[...].astype(BF16)

            @pl.when(zd > z)
            def _():
                z_copy(h, zd, 0).start()

            @pl.when(zd < z)
            def _():
                z_copy(h, zd, 1).start()
        both(d, act)

    def b_steps(h, lo, hi, total):
        def body(i, _):
            @pl.when(i < zn)
            def _():
                y_part(h, zn - 1 - i)

            @pl.when(i >= 1)
            def _():
                z_part(h, zn - i, total)
            return 0
        lax.fori_loop(lo, hi, body, 0)

    def b_drain(h):
        def body(zd, _):
            y_copy(h, zd).wait_send()

            @pl.when(zd > z)
            def _():
                z_copy(h, zd, 0).wait_send()

            @pl.when(zd < z)
            def _():
                z_copy(h, zd, 1).wait_send()
            return 0
        lax.fori_loop(0, zn, body, 0)

    def g1_copy(peer, src):
        return remote(gsend.at[peer], grecv.at[src], g1s.at[peer], g1r.at[src], "col", peer)

    def g2_copy(peer, src):
        return remote(gsum.at[src], gsum.at[src], g2s.at[peer], g2r.at[src], "row", peer)

    def g3_copy(peer, src):
        return remote(gfin.at[src], gfin.at[src], g3s.at[peer], g3r.at[src], "col", peer)

    x_own(0, start)
    tiles[n_tiles] = jnp.zeros((blk, blk), BF16)
    tile_copy.wait()
    per = shard // blk
    n_rows = panel // blk

    def fill(i, _):
        k, row = i // n_rows, i % n_rows
        rows = pl.ds(pl.multiple_of(row * blk, blk), blk)
        for b in range(per):
            slot = slot_ref[row * (nr * per) + k * per + b]
            dense[k, rows, b * blk:(b + 1) * blk] = tiles[slot]
        return 0
    lax.fori_loop(0, nr * n_rows, fill, 0)

    accumulate(0, r, True)
    x_steps(0, 1, zn)
    x_own(1, start)
    x_use(0, zn)
    p_send(0)
    accumulate(1, r, True)
    x_steps(1, 1, 2)

    agg_one = p_sum(0).astype(BF16)
    pre_one = dot(agg_one, w1_ref[...])
    pre[...] = pre_one
    hidden = (pre_one / (1.0 + jnp.exp(-pre_one))).astype(BF16)
    hid[...] = hidden
    z_send(0, dot(hidden, w2_ref[...]))

    x_steps(1, 2, zn)
    x_use(1, zn)
    p_send(1)
    z_wait(0)

    def with_total(total):
        b_steps(0, 0, 2, total)

        agg_grad = p_sum(1).astype(BF16)
        pre_one = pre[...]
        s = 1.0 / (1.0 + jnp.exp(-pre_one))
        slope = s * (1.0 + pre_one * (1.0 - s))
        grad_pre = (dot(agg_grad, w2_ref[...], ((1,), (1,))) * slope).astype(BF16)
        z_send(1, dot(grad_pre, w1_ref[...], ((1,), (1,))))
        one = dot(agg[0].T.astype(BF16), grad_pre) * factor
        two = dot(hid[...].astype(F32).T.astype(BF16), agg_grad) * factor
        for k in range(nc):
            lo = k * piece
            half = one if lo < width else two
            gsend[k] = half[lo % width:lo % width + piece].astype(BF16)
        peers(nc, c, lambda peer: g1_copy(peer, c).start())

        b_steps(0, 2, zn + 1, total)
        out_ref[...] = total[...].T.astype(BF16)

        mine = gsend[c].astype(F32)
        gfin[c] = mine

        def add_piece(peer):
            g1_copy(peer, peer).wait_recv()
            gfin[c] = gfin[c] + grecv[peer].astype(F32)
        peers(nc, c, add_piece)
        gsum[r] = gfin[c].astype(BF16)
        peers(nr, r, lambda peer: g2_copy(peer, r).start())

        z_wait(1)
        b_steps(1, 0, 2, total)

        peers(nr, r, lambda peer: g2_copy(peer, peer).wait_recv())
        gfin[c] = gsum[0].astype(F32)

        def add_row(k, _):
            gfin[c] = gfin[c] + gsum[k].astype(F32)
            return 0
        lax.fori_loop(1, nr, add_row, 0)
        peers(nc, c, lambda peer: g3_copy(peer, c).start())

        b_steps(1, 2, zn + 1, total)
        gf_ref[...] = total[...].T.astype(BF16)

    pl.run_scoped(with_total, pltpu.VMEM((width, shard), F32))

    peers(nc, c, lambda peer: g3_copy(peer, peer).wait_recv())
    for k in range(nc):
        lo = k * piece
        ref = gw1_ref if lo < width else gw2_ref
        ref[lo % width:lo % width + piece, :] = gfin[k]

    for h in range(2):
        x_drain(h)
        peers(nc, c, lambda peer: p_copy(h, peer, c).wait_send())
        peers(nc, c, lambda peer: t_copy(h, peer, c).wait_send())
        b_drain(h)
    peers(nc, c, lambda peer: g1_copy(peer, c).wait_send())
    peers(nr, r, lambda peer: g2_copy(peer, r).wait_send())
    peers(nc, c, lambda peer: g3_copy(peer, c).wait_send())


def on_device(nr, nc, features, weight1, weight2, tile_values, tile_coords, tile_count, out_grad):
    local_tiles = tile_values[0, 0]
    n_tiles, blk = local_tiles.shape[:2]
    shard, width = features.shape[1:]
    panel, col_blocks = shard * nc, shard * nr // blk
    row_blocks = panel // blk
    slots = jnp.arange(n_tiles, dtype=jnp.int32)
    place = tile_coords[0, 0, 0] * col_blocks + tile_coords[0, 0, 1]
    live = slots < tile_count[0, 0]
    hit = (place[None, :] == jnp.arange(row_blocks * col_blocks, dtype=jnp.int32)[:, None]) & live[None, :]
    slot_map = n_tiles + jnp.sum(jnp.where(hit, slots[None, :] - n_tiles, 0), axis=1)
    zn = nr // 2
    piece = 2 * width // nc
    factor = 1.0 / math.sqrt(shard * nr * nc)
    vmem, dma = pltpu.VMEM, pltpu.SemaphoreType.DMA
    in_vmem = pl.BlockSpec(memory_space=pltpu.VMEM)
    output, grad_features, gw1, gw2 = pl.pallas_call(
        functools.partial(kernel, nr, nc, factor),
        out_shape=(
            jax.ShapeDtypeStruct((shard, width), BF16),
            jax.ShapeDtypeStruct((shard, width), BF16),
            jax.ShapeDtypeStruct((width, width), F32),
            jax.ShapeDtypeStruct((width, width), F32),
        ),
        in_specs=[pl.BlockSpec(memory_space=pltpu.SMEM)] + [in_vmem] * 4 + [pl.BlockSpec(memory_space=pl.ANY)],
        out_specs=(in_vmem,) * 4,
        scratch_shapes=[
            vmem((n_tiles + 1, blk, blk), BF16),
            vmem((nr, panel, shard), BF16),
            vmem((2, nr, shard, width), BF16),
            vmem((2, panel, width), F32),
            vmem((2, nc, shard, width), BF16),
            vmem((2, nc, shard, width), BF16),
            vmem((shard, width), F32),
            vmem((shard, width), BF16),
            vmem((2, shard, width), F32),
            vmem((2, nc, width, shard), BF16),
            vmem((2, zn, width, shard), BF16),
            vmem((2, zn, width, shard), BF16),
            vmem((2, zn, width, shard), BF16),
            vmem((2, 2, zn, width, shard), BF16),
            vmem((nc, piece, width), BF16),
            vmem((nc, piece, width), BF16),
            vmem((nr, piece, width), BF16),
            vmem((nc, piece, width), F32),
            dma,
            dma((2, nr, 3)), dma((2, nr)),
            dma((2, nc)), dma((2, nc)),
            dma((2, nc)), dma((2, nc)),
            dma((2, zn)), dma((2, zn)),
            dma((2, zn)), dma((2, 2, zn)),
            dma((nc,)), dma((nc,)),
            dma((nr,)), dma((nr,)),
            dma((nc,)), dma((nc,)),
        ],
        compiler_params=pltpu.CompilerParams(
            collective_id=0, has_side_effects=True, vmem_limit_bytes=56 * 2**20),
    )(slot_map, features[0], out_grad[0], weight1, weight2, local_tiles)
    return output[None], grad_features[None], gw1, gw2


def solution(mesh):
    placed = (
        P("col", "row", None),
        P(),
        P(),
        P("row", "col", None, None, None),
        P("row", "col", None, None),
        P("row", "col"),
        P("col", "row", None),
    )
    return jax.shard_map(
        functools.partial(on_device, mesh.shape["row"], mesh.shape["col"]),
        mesh=mesh,
        in_specs=placed,
        out_specs=(P("col", "row", None), P("col", "row", None), P(), P()),
        check_vma=False,
    )
```

time: 435 us -> 92.6 us (0.21)
  waiting for transfers between devices: 323 us -> 0 us
  Pallas kernels: 0 us -> 83.5 us
  matrix products: 37.9 us -> 0 us
  local copies, waits for them, and re-layouts: 40.7 us -> 6.08 us
  blocking collectives: 15.1 us -> 0 us
  between operations: 14.9 us -> 1.3 us
    reduce_scatter x4 -> x0, waiting for transfers between devices: 135 us -> none  [the longest x1 65.3 us: on_device(): lax.psum_scatter(part_four.astype(jnp.bfloat16), 'row', scatter_dimension...]
    psum x1 -> x0, waiting for transfers between devices: 122 us -> none  [on_device(): sum_one, sum_two = lax.psum((weight_one, weight_two), ('row', 'col'))]
    pallas_call x0 -> x1, Pallas kernels: none -> 83.5 us  [on_device(): pl.pallas_call(functools.partial(kernel, nr, nc, factor), out_shape=(jax....]
    all_gather x2 -> x0, waiting for transfers between devices: 64.4 us -> none  [the longest x1 40.9 us: on_device(): gathered = lax.all_gather(features, 'row', axis=1, tiled=True)[0]]
    dot_general x14 -> x0, matrix products: 37.9 us -> none  [the longest x2 11.8 us: forward_part(): jnp.einsum('tij,tjf->tif', local_tiles, blocks, preferred_element_type=jn...]
    dot_general x4 -> x0, local copies, waits for them, and re-layouts: 19.9 us -> none  [the longest x2 9.98 us: transposed_part(): jnp.einsum('tji,tjf->tif', local_tiles, blocks, preferred_element_type=jn...]
    gather x4 -> x0, local copies, waits for them, and re-layouts: 15.3 us -> none  [the longest x2 7.84 us: forward_part(): blocks = panel_rows.reshape(-1, block_side, feat_width)[col_ids]]
    all_gather x2 -> x0, blocking collectives: 15.1 us -> none  [the longest x1 7.92 us: on_device(): grad_hidden_rows = lax.all_gather(grad_one, 'col', axis=0, tiled=True)]
  transfers between devices with their start and end apart: 7 -> 0, of which waited for: 7 -> 0; matrix products, arithmetic and copies ran while one was open for 14% -> 0% of each run, Pallas kernels for 0% -> 0%
where the time goes in v1:
time: 92.6 us; the launch traced here: 92.3 us
  Pallas kernels  83.5 us (90%)
  local copies, waits for them, and re-layouts  6.08 us (7%)
  other arithmetic  1.48 us (2%)
  between operations  1.3 us (1%)
    pallas_call x1, Pallas kernels, on_device(): pl.pallas_call(functools.partial(kernel, nr, nc, factor), out_shape=(jax....  83.5 us
    unnamed x4, local copies, waits for them, and re-layouts  6.08 us

profile of v1, /device:TPU:0, one launch (start us, length us, event | category | flops | bytes accessed | tf_op | source)
XLA Modules:
  0.0 92.3 jit_solution(5731867952097038875)
XLA Ops:
  1.3 0.8 add_bitcast_fusion
  2.1 0.1 select_reduce_fusion
  2.2 0.6 broadcast_add_fusion.slot_ref
  2.8 83.5 %shard_map.102 = (bf16[512,128]{1,0:T(8,128)(2,1)}, bf16[512,128]{1,0:T(8,128)(2,1)}, f32[128,128]{1,0:T(8,128)}, f32[128,128]{1,0:T(8,128)}) custom-call(s32[512]{0:T(512)} %broadcast_add_fusion.slot_ref, bf16[512,128]{1,0:T(8,128)(2,1)} %bitcast.10, bf16[512,128]{1,0:T(8,128)(2,1)} %bitcast.11, bf16[128,128]{1,0:T(8,128)(2,1)} %w1_ref.1, ...), custom_call_target="tpu_custom_call" | custom-call | tf_op jit(solution)/shard_map/pallas_call | solution.py:404
  86.2 1.6 %copy.16 = bf16[1,512,128]{2,1,0:T(8,128)(2,1)} copy(bf16[1,512,128]{2,1,0:T(8,128)(2,1)} %bitcast.13) | data formatting | bytes 262144
  87.8 1.6 %copy.17 = bf16[1,512,128]{2,1,0:T(8,128)(2,1)} copy(bf16[1,512,128]{2,1,0:T(8,128)(2,1)} %bitcast.12) | data formatting | bytes 262144
  89.4 1.5 %copy.18 = f32[128,128]{1,0:T(8,128)} copy(f32[128,128]{1,0:T(8,128)} %get-tuple-element.18) | data formatting | bytes 131072
  90.8 1.5 %copy.19 = f32[128,128]{1,0:T(8,128)} copy(f32[128,128]{1,0:T(8,128)} %get-tuple-element.19) | data formatting | bytes 131072
  (2 shorter events, 0.0 us)
